TPU v7x, 128 devices: a whole 4x4x4 slice. The times are simulated.
128 devices in a mesh: role: 2 (over y_hi), tile: 64 (over y_lo, x, z, core).
Axes of the slice: x: 4, y: 4 (y_hi: 2, y_lo: 2; y = y_hi * 2 + y_lo), z: 4, core: 2. Of those that a mesh axis runs over, the one named last changes fastest.
Arguments:
- fields_pair: float32 [2, 512, 65536], P('role', None, 'tile'), may hold values from 0 to 1
- velocity: float32 [65536], P('tile'), may hold values from -0.5 to 0.5
- growth: float32 [65536], P('tile'), may hold values from 0.05 to 0.5
- features: bfloat16 [512, 1024], replicated, may hold values from -6 to 6
- assignment: int32 [512], replicated, may hold values from 0 to 511, each once
- out_pair: float32 [2, 1024, 65536], P('role', None, 'tile'), may hold values from -0.1875 to 0.1875
- hidden_pair: float32 [2, 5, 1024, 1024], P('role', None, 'tile'), may hold values from -0.1875 to 0.1875
Outputs:
- fields_next: float32 [2, 512, 65536], P('role', None, 'tile')
- out_next: float32 [2, 1024, 65536], P('role', None, 'tile')
- hidden_next: float32 [2, 5, 1024, 1024], P('role', None, 'tile')
Inputs may be any that keep to these rules, and one draw needn't show every extreme that they name: `assignment`: a permutation of the 512 members.
All inputs are finite; a program needn't handle non-finite values.
Results may differ from a plain program's by a relative error of at most 0.0022.
The roundings to bfloat16 on the way count: a program that leaves them out, or rounds other values in their place, can miss the bound.
Values may be sent and summed in bfloat16 or wider, within the bound.
No kernel may reach another device: no remote copies, remote signals or barrier semaphores. Data moves between devices by JAX's collectives and lax.ppermute only.
A program may use at most 192 MiB of HBM per device.

v0:
```python
import jax
import jax.numpy as jnp
from jax import lax
from jax.sharding import Mesh
from jax.sharding import PartitionSpec as P

BATCH = 512
TILE = ("tile_0", "tile_1", "tile_2", "tile_3")
momentum_decay = 0.9
step_size = 0.1


def extended(value, sides, width):
    for axis, dim in sides:
        count, length = (lax.axis_size(axis), value.shape[dim])
        up = [(i, (i + 1) % count) for i in range(count)]
        down = [(j, i) for i, j in up]
        last = lax.slice_in_dim(value, length - width, length, axis=dim)
        leading = lax.slice_in_dim(value, 0, width, axis=dim)
        before = lax.ppermute(last, axis, up)
        after = lax.ppermute(leading, axis, down)
        value = jnp.concatenate([before, value, after], axis=dim)
    return value


def from_root(value, axis, root):
    return lax.dynamic_index_in_dim(lax.all_gather(value, axis), root, 0, keepdims=False)


def rows_for(lines, count):
    spare = -lines.shape[0] % count
    if not spare:
        return lines
    return jnp.concatenate([lines, jnp.zeros((spare, *lines.shape[1:]), lines.dtype)])


def from_everyone(value, axis):
    copies = jnp.broadcast_to(value, (lax.axis_size(axis), *value.shape))
    return lax.all_to_all(copies, axis, split_axis=0, concat_axis=0, tiled=True)


def joined_along(parts, dim):
    parts = jnp.moveaxis(parts, 0, dim)
    dims = parts.shape
    return parts.reshape(*dims[:dim], dims[dim] * dims[dim + 1], *dims[dim + 2 :])


def gather_axes(value, axes, dim):
    far, near = axes
    parts = from_everyone(from_everyone(value, far), near)
    return joined_along(parts.swapaxes(0, 1).reshape(-1, *value.shape), dim)


def split_up(value, dim, count):
    before, after = (value.shape[:dim], value.shape[dim + 1 :])
    return jnp.moveaxis(value.reshape(*before, count, -1, *after), dim, 0)


def sent_and_summed(value, axis, dim):
    parts = split_up(value, dim, lax.axis_size(axis))
    arrived = lax.all_to_all(parts, axis, split_axis=0, concat_axis=0, tiled=True)
    return arrived.sum(axis=0)


def summed_rows(value, axes, dim):
    far, near = axes
    own = sent_and_summed(split_up(value, dim, lax.axis_size(far)), near, dim + 1)
    return jnp.sum(lax.all_to_all(own, far, 0, 0, tiled=True), axis=0)


def nested_sum(value, axes):
    lines = value.reshape(-1, value.shape[-1])
    padded = rows_for(lines, lax.axis_size(axes[0]) * lax.axis_size(axes[1]))
    whole = gather_axes(summed_rows(padded, axes, 0), axes, 0)
    return lax.slice_in_dim(whole, 0, len(lines)).reshape(value.shape)


def partner(value, axis, distance):
    return lax.ppermute(value, axis, [(i, i ^ 1 << distance) for i in range(lax.axis_size(axis))])


def guarded(flag, action, *operands):

    def skipped(*values):
        return jax.tree.map(jnp.zeros_like, action(*values))

    return lax.cond(flag, action, skipped, *operands)


def silu_slope(values):
    logistic = jax.nn.sigmoid(values)
    return logistic * (1.0 + values * (1.0 - logistic))


def advance(padded, growth):
    states = padded[:-1]
    velocity_row = padded[-1]
    outflow = (
        jnp.maximum(velocity_row[:-1], 0.0) * states[:, :-1]
        + jnp.minimum(velocity_row[:-1], 0.0) * states[:, 1:]
    )
    carried = states[:, 1:-1] - outflow[:, 1:] + outflow[:, :-1]
    return carried + growth * carried * (1.0 - carried)


def body(fields_pair, velocity, growth, features, assignment, out_pair, hidden_pair):
    solver_side = lax.axis_index("role") == 0
    trainer_side = jnp.logical_not(solver_side)
    own_fields = fields_pair[0]
    own_out = out_pair[0]
    own_hidden = hidden_pair[0]
    layer_count = own_hidden.shape[0]
    unit_rows = own_hidden.shape[1]
    first_unit = lax.axis_index(TILE) * unit_rows
    stacked = jnp.concatenate([own_fields, velocity[None, :]], axis=0)
    padded = extended(stacked, ((TILE, 1),), 1)
    advanced = guarded(solver_side, advance, padded, growth)
    fresh_fields = from_root(advanced, "role", 0)
    out_narrow = own_out.astype(jnp.bfloat16)
    hidden_narrow = own_hidden.astype(jnp.bfloat16)
    full_hidden = lax.all_gather(hidden_narrow, TILE, axis=1, tiled=True)

    def forward(features, full_hidden, out_narrow, target):
        inputs = []
        summed_list = []
        activation = features
        for layer_index in range(layer_count):
            inputs.append(activation)
            summed = jnp.dot(
                activation, full_hidden[layer_index], preferred_element_type=jnp.float32
            )
            summed_list.append(summed)
            activation = jax.nn.silu(summed).astype(jnp.bfloat16)
        predicted = jnp.dot(activation, out_narrow, preferred_element_type=jnp.float32)
        residual = ((predicted - target) / BATCH).astype(jnp.bfloat16)
        grad_out = jnp.dot(activation.T, residual, preferred_element_type=jnp.float32)
        partial_grad = lax.dot_general(
            residual, out_narrow, (((1,), (1,)), ((), ())), preferred_element_type=jnp.float32
        )
        return (jnp.stack(summed_list), jnp.stack(inputs), grad_out, partial_grad)

    summed_all, inputs_all, grad_out, partial_grad = guarded(
        trainer_side, forward, features, full_hidden, out_narrow, own_fields
    )
    upstream = nested_sum(partial_grad, (("tile_0", "tile_1", "tile_2"), "tile_3"))

    def backward(summed_all, inputs_all, upstream, full_hidden, first_unit):
        gradients = []
        for layer_index in reversed(range(layer_count)):
            slope = (upstream * silu_slope(summed_all[layer_index])).astype(jnp.bfloat16)
            own_inputs = lax.dynamic_slice_in_dim(inputs_all[layer_index], first_unit, unit_rows, 1)
            gradients.append(jnp.dot(own_inputs.T, slope, preferred_element_type=jnp.float32))
            if layer_index > 0:
                upstream = lax.dot_general(
                    slope,
                    full_hidden[layer_index],
                    (((1,), (1,)), ((), ())),
                    preferred_element_type=jnp.float32,
                )
        return jnp.stack(gradients[::-1])

    grad_hidden = guarded(
        trainer_side, backward, summed_all, inputs_all, upstream, full_hidden, first_unit
    )
    solver_pack = jnp.concatenate([own_out.reshape(-1), own_hidden.reshape(-1)])
    trainer_pack = jnp.concatenate([grad_out.reshape(-1), grad_hidden.reshape(-1)])
    payload = jnp.where(solver_side, solver_pack, trainer_pack)
    received = partner(payload, "role", 0)
    out_length = own_out.size
    other_out = received[:out_length].reshape(own_out.shape)
    other_hidden = received[out_length:].reshape(own_hidden.shape)
    out_next = jnp.where(
        solver_side,
        momentum_decay * own_out + other_out,
        own_out - step_size * (momentum_decay * other_out + grad_out),
    )
    hidden_next = jnp.where(
        solver_side,
        momentum_decay * own_hidden + other_hidden,
        own_hidden - step_size * (momentum_decay * other_hidden + grad_hidden),
    )
    fields_next = jnp.where(solver_side, advanced, jnp.take(fresh_fields, assignment, axis=0))
    return (fields_next[None], out_next[None], hidden_next[None])


def solution(mesh):
    finer = Mesh(
        mesh.devices.reshape(mesh.shape["role"], 2, 4, 4, 2),
        ("role", "tile_0", "tile_1", "tile_2", "tile_3"),
    )
    in_specs = (
        P("role", None, TILE),
        P(TILE),
        P(TILE),
        P(),
        P(),
        P("role", None, TILE),
        P("role", None, TILE, None),
    )
    out_specs = (P("role", None, TILE), P("role", None, TILE), P("role", None, TILE, None))
    return jax.shard_map(body, mesh=finer, in_specs=in_specs, out_specs=out_specs, check_vma=False)
```

profile of v0, /device:TPU:1, one launch (start us, length us, event | category | flops | bytes accessed | tf_op | source)
XLA Modules:
  0.0 405.7 jit_solution(4291175389253201771)
XLA Ops:
  9.7 119.9 %all-gather.4.cloned.1.call-done = bf16[5,1024,1024]{2,1,0:T(8,128)(2,1)} async-done(((bf16[5,16,1024]{2,1,0:T(8,128)(2,1)}), bf16[5,1024,1024]{2,1,0:T(8,128)(2,1)}) %all-gather.4.cloned.1.call-update) | async-done | bytes 10485776 | tf_op jit(solution)/shard_map/all_gather | solution.py:121
  129.7 11.4 %conditional.4 = (f32[5,512,1024]{2,1,0:T(8,128)}, bf16[5,512,1024]{2,1,0:T(8,128)(2,1)}, f32[1024,1024]{1,0:T(8,128)}, f32[512,1024]{1,0:T(8,128)S(1)}, f32[1048576]{0:T(1024)S(1)}) conditional(s32[]{:T(128)} %convert_element_type.57, () %tuple.54, (bf16[5,1024,1024]{2,1,0:T(8,128)(2,1)}, bf16[512,1024]{1,0:T(8,128)(2,1)}, f32[1024,1024]{1,0:T(8,128)}, ...), branch_computations={%region_2.3_spmd, %region_3.4_spmd} | conditional | flops 8619819008 | bytes 165675232 | solution.py:87
  129.7 5.2 %broadcast.54 = f32[5,512,1024]{2,1,0:T(8,128)} broadcast(f32[]{:T(128)} %constant.80.clone), dimensions={} | broadcast | bytes 10485764 | tf_op jit(solution)/shard_map/broadcast.15
  134.9 3.0 broadcast.55
  137.9 2.5 broadcast.56
  143.2 5.3 %all_to_all.20 = f32[2,32,8,1024]{3,2,1,0:T(8,128)S(1)} all-to-all(f32[2,32,8,1024]{3,2,1,0:T(8,128)S(1)} %copy.15), channel_id=1, replica_groups=mesh['role'=2,'tile_0'=2,'tile_1'=4,'tile_2'=4,'tile_3'=2] {'tile_3'}, dimensions={0} | all-to-all | bytes 4194304 | tf_op jit(solution)/shard_map/all_to_all | solution.py:61
  149.7 21.2 %all_to_all.21 = f32[32,8,1024]{2,1,0:T(8,128)S(1)} all-to-all(f32[32,8,1024]{2,1,0:T(8,128)} %reduce_sum.18), channel_id=1, replica_groups=mesh['role'=2,'tile_0'=2,'tile_1'=4,'tile_2'=4,'tile_3'=2] {'tile_0','ti..., dimensions={0} | all-to-all | bytes 2097152 | tf_op jit(solution)/shard_map/all_to_all | solution.py:68
  172.1 4.7 %all-to-all-start.2 = ((f32[32,8,1024]{2,1,0:T(8,128)}), f32[32,8,1024]{2,1,0:T(8,128)S(1)}, u32[]{:S(2)}, u32[]{:S(2)}) async-start(f32[32,8,1024]{2,1,0:T(8,128)} %broadcast_in_dim.38), calls=%async_computation.2 | async-start | bytes 2097152 | tf_op jit(solution)/shard_map/all_to_all | solution.py:39
  177.8 3.4 collective-permute-start
  182.6 5.2 %copy.19 = f32[128,8,8,128]{3,1,2,0:T(8,128)} copy(f32[128,8,8,128]{3,2,1,0:T(8,128)} %bitcast.227) | data formatting | bytes 8388608
  188.6 3.5 collective-permute-done
  194.6 3.1 concatenate.13
  197.6 3.2 conditional.3
  198.4 2.5 multiply_add_fusion.1
  201.2 9.4 %all_to_all.22 = f32[2,32,8,1024]{3,2,1,0:T(8,128)S(1)} all-to-all(f32[2,32,8,1024]{3,2,1,0:T(8,128)S(1)} %broadcast_in_dim.39), channel_id=1, replica_groups=mesh['role'=2,'tile_0'=2,'tile_1'=4,'tile_2'=4,'tile_3'=2] {'tile_3'}, dimensions={0} | all-to-all | bytes 4194304 | tf_op jit(solution)/shard_map/all_to_all | solution.py:39
  212.1 5.7 %maximum_select_fusion = f32[1130496]{0:T(1024)} fusion(f32[81920]{0:T(1024)S(1)} %bitcast.240, f32[1048576]{0:T(1024)} %bitcast.229, f32[81920]{0:T(1024)} %get-tuple-element.91, f32[1048576]{0:T(1024)} %copy-done.2, pred[]{:T(512)S(6)} %eq.3), kind=kLoop, calls=%fused_computation.118 | loop fusion | flops 3391488 | bytes 13565953 | tf_op jit(solution)/shard_map/jit(_where)/select_n | solution.py:167
  217.9 53.5 %collective-permute-start.2 = (f32[1130496]{0:T(1024)}, f32[1130496]{0:T(1024)}, u32[]{:S(2)}, u32[]{:S(2)}) collective-permute-start(f32[1130496]{0:T(1024)} %maximum_select_fusion), channel_id=1, source_target_pairs={{0,64},{64,0},{1,65},{65,1},{2,66},{66,2},{3,67},{67,3},{4,68},{68... | collective-permute-start | bytes 13565960 | tf_op jit(solution)/shard_map/ppermute | solution.py:79
  271.4 15.9 %all-gather.6.cloned.1.call-done = f32[1024,1024]{1,0:T(8,128)} async-done(((f32[512,1024]{1,0:T(8,128)}), f32[1024,1024]{1,0:T(8,128)}) %all-gather.6.cloned.1.call-update) | async-done | bytes 4194320 | tf_op jit(solution)/shard_map/all_gather | solution.py:27
  288.9 2.7 gather_fusion
  291.6 3.8 select_bitcast_fusion.1
  295.4 81.9 %collective-permute-done.2 = f32[1130496]{0:T(1024)} collective-permute-done((f32[1130496]{0:T(1024)}, f32[1130496]{0:T(1024)}, u32[]{:S(2)}, u32[]{:S(2)}) %collective-permute-start.2) | collective-permute-done | bytes 4522016 | tf_op jit(solution)/shard_map/ppermute | solution.py:79
  378.3 4.4 %slice.146 = f32[1048576]{0:T(1024)} slice(f32[1130496]{0:T(1024)} %collective-permute-done.2), slice={[0:1048576]} | slice | bytes 8388608 | tf_op jit(solution)/shard_map/slice | solution.py:170
  382.7 5.0 %slice.133 = f32[1024,1024]{1,0:T(8,128)} reshape(f32[1048576]{0:T(1024)} %slice.146) | data formatting | bytes 8388608 | tf_op jit(solution)/shard_map/slice | solution.py:170
  389.5 8.7 %select_bitcast_fusion = f32[1,1024,1024]{2,1,0:T(8,128)} fusion(f32[1024,1024]{1,0:T(8,128)} %get-tuple-element.92, f32[1024,1024]{1,0:T(8,128)} %slice.133, pred[]{:T(512)S(6)} %eq.3, f32[1,1024,1024]{2,1,0:T(8,128)} %param.18), kind=kLoop, calls=%fused_computation.119 | loop fusion | flops 7340032 | bytes 16777216 | tf_op jit(solution)/shard_map/broadcast_in_dim | solution.py:183
  (49 shorter events, 20.8 us)
Async XLA Ops:
  8.0 121.7 %all-gather.4.cloned.1.call-start = ((), (), s32[]{:S(2)}) async-start(), calls=%async_computation.4 | async-start | bytes 10649600 | tf_op jit(solution)/shard_map/all_gather | solution.py:121
  141.1 2.1 copy-start.2
  170.9 5.9 %copy-start.3 = (f32[1,512,1024]{2,1,0:T(8,128)S(1)}, f32[1,512,1024]{2,1,0:T(8,128)}, u32[]{:S(2)}) copy-start(f32[1,512,1024]{2,1,0:T(8,128)} %param.13) | copy-start | bytes 6291460
  170.9 5.9 %copy-start.13 = (f32[1024]{0:T(1024)S(1)}, f32[1024]{0:T(1024)}, u32[]{:S(2)}) copy-start(f32[1024]{0:T(1024)} %param.14) | copy-start | bytes 12292
  172.1 28.8 %all-to-all-start.2 = ((f32[32,8,1024]{2,1,0:T(8,128)}), f32[32,8,1024]{2,1,0:T(8,128)S(1)}, u32[]{:S(2)}, u32[]{:S(2)}) async-start(f32[32,8,1024]{2,1,0:T(8,128)} %broadcast_in_dim.38), calls=%async_computation.2 | async-start | bytes 2097152 | tf_op jit(solution)/shard_map/all_to_all | solution.py:39
  176.8 110.5 %all-gather.6.cloned.1.call-start = ((), (), s32[]{:S(2)}) async-start(), calls=%async_computation.5 | async-start | bytes 6291456 | tf_op jit(solution)/shard_map/all_gather | solution.py:27
  177.8 14.3 %collective-permute-start = (f32[513,1]{1,0:T(8,128)}, f32[513,1]{1,0:T(8,128)S(1)}, u32[]{:S(2)}, u32[]{:S(2)}) collective-permute-start(f32[513,1]{1,0:T(8,128)} %get-tuple-element.140), channel_id=1, source_target_pairs={{0,1},{1,2},{2,3},{3,4},{4,5},{5,6},{6,7},{7,8},{8,9},{9,10},{10,1... | collective-permute-start | bytes 6164 | tf_op jit(solution)/shard_map/ppermute | solution.py:20
  181.1 13.4 %collective-permute-start.1 = (f32[513,1]{1,0:T(8,128)}, f32[513,1]{1,0:T(8,128)}, u32[]{:S(2)}, u32[]{:S(2)}) collective-permute-start(f32[513,1]{1,0:T(8,128)} %get-tuple-element.139), channel_id=1, source_target_pairs={{1,0},{2,1},{3,2},{4,3},{5,4},{6,5},{7,6},{8,7},{9,8},{10,9},{11,1... | collective-permute-start | bytes 6164 | tf_op jit(solution)/shard_map/ppermute | solution.py:21
  182.6 5.2 %copy-start.5 = (f32[1,5,16,1024]{3,2,1,0:T(8,128)S(1)}, f32[1,5,16,1024]{3,2,1,0:T(8,128)}, u32[]{:S(2)}) copy-start(f32[1,5,16,1024]{3,2,1,0:T(8,128)} %param.19) | copy-start | bytes 983044
  188.6 9.1 %copy-start.15 = (f32[1024]{0:T(1024)S(1)}, f32[1024]{0:T(1024)}, u32[]{:S(2)}) copy-start(f32[1024]{0:T(1024)} %param.15) | copy-start | bytes 12292
  192.1 0.7 copy-start.12
  210.6 1.5 copy-start.7
  212.1 59.3 %copy-start.14 = (s32[512]{0:T(512)S(1)}, s32[512]{0:T(512)}, u32[]{:S(2)}) copy-start(s32[512]{0:T(512)} %param.17) | copy-start | bytes 6148
  217.9 159.4 %collective-permute-start.2 = (f32[1130496]{0:T(1024)}, f32[1130496]{0:T(1024)}, u32[]{:S(2)}, u32[]{:S(2)}) collective-permute-start(f32[1130496]{0:T(1024)} %maximum_select_fusion), channel_id=1, source_target_pairs={{0,64},{64,0},{1,65},{65,1},{2,66},{66,2},{3,67},{67,3},{4,68},{68... | collective-permute-start | bytes 13565960 | tf_op jit(solution)/shard_map/ppermute | solution.py:79
  287.3 1.6 slice-start
  382.7 5.0 %copy-start.6 = (f32[1,5,16,1024]{3,2,1,0:T(8,128)S(1)}, f32[1,5,16,1024]{3,2,1,0:T(8,128)}, u32[]{:S(2)}) copy-start(f32[1,5,16,1024]{3,2,1,0:T(8,128)} %param.19) | copy-start | bytes 983044
Sparse Core Ops, SparseCore 0:
  11.1 118.5 all-gather.3
Sparse Core Ops, SparseCore 1:
  201.0 86.3 all-gather.5
where the time goes:
time: 407 us; the launch traced here: 406 us
  waiting for transfers between devices  223 us (55%)
  starting transfers between devices  61.7 us (15%)
  local copies, waits for them, and re-layouts  40.8 us (10%)
  blocking collectives  35.9 us (9%)
  other arithmetic  28.5 us (7%)
  between operations  15.6 us (4%)
    all_gather x1, waiting for transfers between devices, body(): full_hidden = lax.all_gather(hidden_narrow, TILE, axis=1, tiled=True)  120 us
    ppermute x1, waiting for transfers between devices, partner(): lax.ppermute(value, axis, [(i, i ^ 1 << distance) for i in range(lax.axis...  81.9 us
    ppermute x1, starting transfers between devices, partner(): lax.ppermute(value, axis, [(i, i ^ 1 << distance) for i in range(lax.axis...  53.5 us
    all_to_all x1, blocking collectives, summed_rows(): return jnp.sum(lax.all_to_all(own, far, 0, 0, tiled=True), axis=0)  21.2 us
    all_gather x1, waiting for transfers between devices, from_root(): lax.all_gather(value, axis)  15.9 us
    broadcast_in_dim x3, other arithmetic, body(): return (fields_next[None], out_next[None], hidden_next[None])  14.3 us
    another operation x5, local copies, waits for them, and re-layouts  11.7 us
    slice x2, local copies, waits for them, and re-layouts, body(): other_out = received[:out_length].reshape(own_out.shape)  9.46 us
  transfers between devices with their start and end apart: 6, of which 5 were waited for; matrix products, arithmetic and copies ran while one was open for 7% of the time, Pallas kernels for 0%

commit v1 on v0

--- a/solution.py
+++ b/solution.py
@@ -118,7 +118,8 @@
     fresh_fields = from_root(advanced, "role", 0)
     out_narrow = own_out.astype(jnp.bfloat16)
     hidden_narrow = own_hidden.astype(jnp.bfloat16)
-    full_hidden = lax.all_gather(hidden_narrow, TILE, axis=1, tiled=True)
+    sent = jnp.stack([hidden_narrow] * lax.axis_size(TILE))
+    full_hidden = jnp.concatenate(lax.all_to_all(sent, TILE, 0, 0), axis=1)
 
     def forward(features, full_hidden, out_narrow, target):
         inputs = []

time: 407 us -> 464 us (1.14)
  local copies, waits for them, and re-layouts: 40.8 us -> 56.6 us
  waiting for transfers between devices: 223 us -> 238 us
  blocking collectives: 35.9 us -> 48.6 us
  loops' own time: 0.23 us -> 5.68 us
  starting transfers between devices: 61.7 us -> 66.8 us
    all_to_all x0 -> x1, waiting for transfers between devices: none -> 135 us  [body(): full_hidden = jnp.concatenate(lax.all_to_all(sent, TILE, 0, 0), axis=1)]
    all_gather x1 -> x0, waiting for transfers between devices: 120 us -> none  [body(): full_hidden = lax.all_gather(hidden_narrow, TILE, axis=1, tiled=True)]
    all_to_all x1, blocking collectives: 21.2 us -> 33.3 us  [summed_rows(): return jnp.sum(lax.all_to_all(own, far, 0, 0, tiled=True), axis=0)]
    all_to_all x0 -> x1, starting transfers between devices: none -> 11 us  [body(): full_hidden = jnp.concatenate(lax.all_to_all(sent, TILE, 0, 0), axis=1)]
    all_to_all x0 -> x1, local copies, waits for them, and re-layouts: none -> 10.4 us  [body(): full_hidden = jnp.concatenate(lax.all_to_all(sent, TILE, 0, 0), axis=1)]
    ppermute x1, starting transfers between devices: 53.5 us -> 47.7 us  [partner(): lax.ppermute(value, axis, [(i, i ^ 1 << distance) for i in range(lax.axis...]
    another operation x3, loops' own time: 0.23 us -> 5.68 us  [guarded(): return lax.cond(flag, action, skipped, *operands)]
    another operation x5 -> x6, local copies, waits for them, and re-layouts: 11.7 us -> 17.1 us
  transfers between devices with their start and end apart: 6 -> 6, of which waited for: 5 -> 5; matrix products, arithmetic and copies ran while one was open for 7% -> 6% of each run, Pallas kernels for 0% -> 0%
where the time goes in v1:
time: 464 us; the launch traced here: 459 us
  waiting for transfers between devices  238 us (51%)
  starting transfers between devices  66.8 us (14%)
  local copies, waits for them, and re-layouts  56.6 us (12%)
  blocking collectives  48.6 us (10%)
  other arithmetic  29.5 us (6%)
  between operations  14.4 us (3%)
  loops' own time  5.68 us (1%)
    all_to_all x1, waiting for transfers between devices, body(): full_hidden = jnp.concatenate(lax.all_to_all(sent, TILE, 0, 0), axis=1)  135 us
    ppermute x1, waiting for transfers between devices, partner(): lax.ppermute(value, axis, [(i, i ^ 1 << distance) for i in range(lax.axis...  81.7 us
    ppermute x1, starting transfers between devices, partner(): lax.ppermute(value, axis, [(i, i ^ 1 << distance) for i in range(lax.axis...  47.7 us
    all_to_all x1, blocking collectives, summed_rows(): return jnp.sum(lax.all_to_all(own, far, 0, 0, tiled=True), axis=0)  33.3 us
    all_gather x1, waiting for transfers between devices, from_root(): lax.all_gather(value, axis)  16 us
    broadcast_in_dim x3, other arithmetic, body(): return (fields_next[None], out_next[None], hidden_next[None])  14.3 us
    another operation x5, local copies, waits for them, and re-layouts  11.7 us
    all_to_all x1, starting transfers between devices, body(): full_hidden = jnp.concatenate(lax.all_to_all(sent, TILE, 0, 0), axis=1)  11 us
  transfers between devices with their start and end apart: 6, of which 5 were waited for; matrix products, arithmetic and copies ran while one was open for 6% of the time, Pallas kernels for 0%

profile of v1, /device:TPU:1, one launch (start us, length us, event | category | flops | bytes accessed | tf_op | source)
XLA Modules:
  0.0 459.3 jit_solution(1391987299070624361)
XLA Ops:
  8.2 5.4 %stack.47 = bf16[64,5,16,1024]{3,2,1,0:T(8,128)(2,1)} broadcast(bf16[5,16,1024]{2,1,0:T(8,128)(2,1)S(1)} %convert_bitcast_fusion), dimensions={1,2,3} | broadcast | bytes 10649600 | tf_op jit(solution)/shard_map/stack | solution.py:121
  13.5 11.0 %all-to-all-start = ((bf16[64,5,16,1024]{3,2,1,0:T(8,128)(2,1)}), bf16[64,5,16,1024]{3,2,1,0:T(8,128)(2,1)}, u32[]{:S(2)}, u32[]{:S(2)}) async-start(bf16[64,5,16,1024]{3,2,1,0:T(8,128)(2,1)} %stack.47), calls=%async_computation | async-start | bytes 20971520 | tf_op jit(solution)/shard_map/all_to_all | solution.py:122
  24.6 134.8 %all-to-all-done = bf16[64,5,16,1024]{3,2,1,0:T(8,128)(2,1)} async-done(((bf16[64,5,16,1024]{3,2,1,0:T(8,128)(2,1)}), bf16[64,5,16,1024]{3,2,1,0:T(8,128)(2,1)}, u32[]{:S(2)}, u32[]{:S(2)}) %all-to-all-start) | async-done | bytes 10485792 | tf_op jit(solution)/shard_map/all_to_all | solution.py:122
  159.3 10.4 %copy.16 = bf16[64,5,16,1024]{3,2,0,1:T(8,128)(2,1)} copy(bf16[64,5,16,1024]{3,2,1,0:T(8,128)(2,1)} %all-to-all-done) | data formatting | bytes 20971520 | tf_op jit(solution)/shard_map/all_to_all | solution.py:122
  169.8 16.8 %conditional.4 = (f32[5,512,1024]{2,1,0:T(8,128)}, bf16[5,512,1024]{2,1,0:T(8,128)(2,1)}, f32[1024,1024]{1,0:T(8,128)}, f32[512,1024]{1,0:T(8,128)S(1)}, f32[1048576]{0:T(1024)S(1)}) conditional(s32[]{:T(128)} %convert_element_type.58, () %tuple.54, (bf16[5,1024,1024]{2,1,0:T(8,128)(2,1)}, bf16[512,1024]{1,0:T(8,128)(2,1)S(1)}, ...), branch_computations={%region_2.3_spmd, %region_3.4_spmd} | conditional | flops 8619819008 | bytes 153092256 | solution.py:87
  169.8 5.2 %broadcast.55 = f32[5,512,1024]{2,1,0:T(8,128)} broadcast(f32[]{:T(128)} %constant.80.clone), dimensions={} | broadcast | bytes 10485764 | tf_op jit(solution)/shard_map/broadcast.15
  175.0 3.0 broadcast.56
  188.6 5.9 %all_to_all.25 = f32[2,32,8,1024]{3,2,1,0:T(8,128)} all-to-all(f32[2,32,8,1024]{3,2,1,0:T(8,128)S(1)} %copy.17), channel_id=1, replica_groups=mesh['role'=2,'tile_0'=2,'tile_1'=4,'tile_2'=4,'tile_3'=2] {'tile_3'}, dimensions={0} | all-to-all | bytes 4194304 | tf_op jit(solution)/shard_map/all_to_all | solution.py:61
  197.4 33.3 %all_to_all.26 = f32[32,8,1024]{2,1,0:T(8,128)S(1)} all-to-all(f32[32,8,1024]{2,1,0:T(8,128)} %reduce_sum.18), channel_id=1, replica_groups=mesh['role'=2,'tile_0'=2,'tile_1'=4,'tile_2'=4,'tile_3'=2] {'tile_0','ti..., dimensions={0} | all-to-all | bytes 2097152 | tf_op jit(solution)/shard_map/all_to_all | solution.py:68
  231.8 4.7 %all-to-all-start.3 = ((f32[32,8,1024]{2,1,0:T(8,128)}), f32[32,8,1024]{2,1,0:T(8,128)S(1)}, u32[]{:S(2)}, u32[]{:S(2)}) async-start(f32[32,8,1024]{2,1,0:T(8,128)} %broadcast_in_dim.38), calls=%async_computation.3 | async-start | bytes 2097152 | tf_op jit(solution)/shard_map/all_to_all | solution.py:39
  237.5 3.4 collective-permute-start
  242.3 5.2 %copy.21 = f32[128,8,8,128]{3,1,2,0:T(8,128)} copy(f32[128,8,8,128]{3,2,1,0:T(8,128)} %bitcast.231) | data formatting | bytes 8388608
  248.3 3.5 collective-permute-done
  254.3 3.1 concatenate.13
  257.4 3.2 conditional.3
  260.9 9.4 %all_to_all.27 = f32[2,32,8,1024]{3,2,1,0:T(8,128)S(1)} all-to-all(f32[2,32,8,1024]{3,2,1,0:T(8,128)S(1)} %broadcast_in_dim.39), channel_id=1, replica_groups=mesh['role'=2,'tile_0'=2,'tile_1'=4,'tile_2'=4,'tile_3'=2] {'tile_3'}, dimensions={0} | all-to-all | bytes 4194304 | tf_op jit(solution)/shard_map/all_to_all | solution.py:39
  272.0 5.7 %maximum_select_fusion = f32[1130496]{0:T(1024)} fusion(f32[81920]{0:T(1024)S(1)} %bitcast.248, f32[1048576]{0:T(1024)} %bitcast.233, f32[81920]{0:T(1024)} %get-tuple-element.91, f32[1048576]{0:T(1024)} %copy-done.2, pred[]{:T(512)S(6)} %eq.3), kind=kLoop, calls=%fused_computation.118 | loop fusion | flops 3391488 | bytes 13565953 | tf_op jit(solution)/shard_map/jit(_where)/select_n | solution.py:168
  277.7 47.7 %collective-permute-start.2 = (f32[1130496]{0:T(1024)}, f32[1130496]{0:T(1024)}, u32[]{:S(2)}, u32[]{:S(2)}) collective-permute-start(f32[1130496]{0:T(1024)} %maximum_select_fusion), channel_id=1, source_target_pairs={{0,64},{64,0},{1,65},{65,1},{2,66},{66,2},{3,67},{67,3},{4,68},{68... | collective-permute-start | bytes 13565960 | tf_op jit(solution)/shard_map/ppermute | solution.py:79
  325.4 16.0 %all-gather.3.cloned.1.call-done = f32[1024,1024]{1,0:T(8,128)} async-done(((f32[512,1024]{1,0:T(8,128)}), f32[1024,1024]{1,0:T(8,128)}) %all-gather.3.cloned.1.call-update) | async-done | bytes 4194320 | tf_op jit(solution)/shard_map/all_gather | solution.py:27
  345.6 3.8 select_bitcast_fusion.1
  349.5 81.7 %collective-permute-done.2 = f32[1130496]{0:T(1024)} collective-permute-done((f32[1130496]{0:T(1024)}, f32[1130496]{0:T(1024)}, u32[]{:S(2)}, u32[]{:S(2)}) %collective-permute-start.2) | collective-permute-done | bytes 4522016 | tf_op jit(solution)/shard_map/ppermute | solution.py:79
  432.2 4.4 slice.146
  436.7 5.0 %slice.133 = f32[1024,1024]{1,0:T(8,128)} reshape(f32[1048576]{0:T(1024)} %slice.146) | data formatting | bytes 8388608 | tf_op jit(solution)/shard_map/slice | solution.py:171
  443.5 8.7 %select_bitcast_fusion = f32[1,1024,1024]{2,1,0:T(8,128)} fusion(f32[1024,1024]{1,0:T(8,128)} %get-tuple-element.92, f32[1024,1024]{1,0:T(8,128)} %slice.133, pred[]{:T(512)S(6)} %eq.3, f32[1,1024,1024]{2,1,0:T(8,128)} %param.18), kind=kLoop, calls=%fused_computation.119 | loop fusion | flops 7340032 | bytes 16777216 | tf_op jit(solution)/shard_map/broadcast_in_dim | solution.py:184
  (52 shorter events, 29.6 us)
Async XLA Ops:
  13.5 145.8 %all-to-all-start = ((bf16[64,5,16,1024]{3,2,1,0:T(8,128)(2,1)}), bf16[64,5,16,1024]{3,2,1,0:T(8,128)(2,1)}, u32[]{:S(2)}, u32[]{:S(2)}) async-start(bf16[64,5,16,1024]{3,2,1,0:T(8,128)(2,1)} %stack.47), calls=%async_computation | async-start | bytes 20971520 | tf_op jit(solution)/shard_map/all_to_all | solution.py:122
  24.5 145.2 %copy-start.3 = (f32[1,512,1024]{2,1,0:T(8,128)S(1)}, f32[1,512,1024]{2,1,0:T(8,128)}, u32[]{:S(2)}) copy-start(f32[1,512,1024]{2,1,0:T(8,128)} %param.13) | copy-start | bytes 6291460
  24.6 145.2 %copy-start.7 = (bf16[512,1024]{1,0:T(8,128)(2,1)S(1)}, bf16[512,1024]{1,0:T(8,128)(2,1)}, u32[]{:S(2)}) copy-start(bf16[512,1024]{1,0:T(8,128)(2,1)} %param.16) | copy-start | bytes 3145732
  186.5 2.1 copy-start.2
  230.7 5.9 %copy-start.12 = (f32[1024]{0:T(1024)S(1)}, f32[1024]{0:T(1024)}, u32[]{:S(2)}) copy-start(f32[1024]{0:T(1024)} %param.14) | copy-start | bytes 12292
  231.8 28.8 %all-to-all-start.3 = ((f32[32,8,1024]{2,1,0:T(8,128)}), f32[32,8,1024]{2,1,0:T(8,128)S(1)}, u32[]{:S(2)}, u32[]{:S(2)}) async-start(f32[32,8,1024]{2,1,0:T(8,128)} %broadcast_in_dim.38), calls=%async_computation.3 | async-start | bytes 2097152 | tf_op jit(solution)/shard_map/all_to_all | solution.py:39
  236.6 104.8 %all-gather.3.cloned.1.call-start = ((), (), s32[]{:S(2)}) async-start(), calls=%async_computation.5 | async-start | bytes 6291456 | tf_op jit(solution)/shard_map/all_gather | solution.py:27
  237.5 14.3 %collective-permute-start = (f32[513,1]{1,0:T(8,128)}, f32[513,1]{1,0:T(8,128)S(1)}, u32[]{:S(2)}, u32[]{:S(2)}) collective-permute-start(f32[513,1]{1,0:T(8,128)} %get-tuple-element.140), channel_id=1, source_target_pairs={{0,1},{1,2},{2,3},{3,4},{4,5},{5,6},{6,7},{7,8},{8,9},{9,10},{10,1... | collective-permute-start | bytes 6164 | tf_op jit(solution)/shard_map/ppermute | solution.py:20
  240.8 13.5 %collective-permute-start.1 = (f32[513,1]{1,0:T(8,128)}, f32[513,1]{1,0:T(8,128)}, u32[]{:S(2)}, u32[]{:S(2)}) collective-permute-start(f32[513,1]{1,0:T(8,128)} %get-tuple-element.139), channel_id=1, source_target_pairs={{1,0},{2,1},{3,2},{4,3},{5,4},{6,5},{7,6},{8,7},{9,8},{10,9},{11,1... | collective-permute-start | bytes 6164 | tf_op jit(solution)/shard_map/ppermute | solution.py:21
  242.3 5.2 %copy-start.4 = (f32[1,5,16,1024]{3,2,1,0:T(8,128)S(1)}, f32[1,5,16,1024]{3,2,1,0:T(8,128)}, u32[]{:S(2)}) copy-start(f32[1,5,16,1024]{3,2,1,0:T(8,128)} %param.19) | copy-start | bytes 983044
  248.3 9.1 %copy-start.14 = (f32[1024]{0:T(1024)S(1)}, f32[1024]{0:T(1024)}, u32[]{:S(2)}) copy-start(f32[1024]{0:T(1024)} %param.15) | copy-start | bytes 12292
  251.8 0.7 copy-start.11
  270.3 1.7 copy-start.6
  272.0 53.4 %copy-start.13 = (s32[512]{0:T(512)S(1)}, s32[512]{0:T(512)}, u32[]{:S(2)}) copy-start(s32[512]{0:T(512)} %param.17) | copy-start | bytes 6148
  277.7 153.4 %collective-permute-start.2 = (f32[1130496]{0:T(1024)}, f32[1130496]{0:T(1024)}, u32[]{:S(2)}, u32[]{:S(2)}) collective-permute-start(f32[1130496]{0:T(1024)} %maximum_select_fusion), channel_id=1, source_target_pairs={{0,64},{64,0},{1,65},{65,1},{2,66},{66,2},{3,67},{67,3},{4,68},{68... | collective-permute-start | bytes 13565960 | tf_op jit(solution)/shard_map/ppermute | solution.py:79
  341.4 1.6 slice-start
  436.7 5.0 %copy-start.5 = (f32[1,5,16,1024]{3,2,1,0:T(8,128)S(1)}, f32[1,5,16,1024]{3,2,1,0:T(8,128)}, u32[]{:S(2)}) copy-start(f32[1,5,16,1024]{3,2,1,0:T(8,128)} %param.19) | copy-start | bytes 983044
Sparse Core Ops, SparseCore 0:
  260.7 80.6 all-gather.2
